TPU v7x, 32 devices: a whole 2x2x4 slice. The times are simulated.
32 devices in a mesh: rep: 8 (over y, x, core), shard: 4 (over z).
Axes of the slice: x: 2, y: 2, z: 4, core: 2. Of those that a mesh axis runs over, the one named last changes fastest.
Arguments:
- grads_matrix: bfloat16 [8, 4, 3, 1024, 1024], P('rep', 'shard'), may hold values from -400 to 400
- grads_vector: bfloat16 [8, 4, 5, 1024], P('rep', 'shard'), may hold values from -6 to 6
- master_matrix: float32 [3, 1024, 1024], P(None, 'shard'), may hold values from -0.1875 to 0.1875
- master_vector: float32 [5, 1024], P(None, 'shard'), may hold values from 0.5 to 1.5
- moment_matrix: float32 [3, 1024, 1024], P(None, 'shard'), may hold values from -4 to 4
- moment_vector: float32 [5, 1024], P(None, 'shard'), may hold values from -4 to 4
- second_matrix: float32 [3, 1024, 1024], P(None, 'shard'), may hold values from 0.05 to 2
- second_vector: float32 [5, 1024], P(None, 'shard'), may hold values from 0.05 to 2
Outputs:
- matrix_master: float32 [3, 1024, 1024], P(None, 'shard')
- vector_master: float32 [5, 1024], P(None, 'shard')
- matrix_moment: float32 [3, 1024, 1024], P(None, 'shard')
- vector_moment: float32 [5, 1024], P(None, 'shard')
- matrix_second: float32 [3, 1024, 1024], P(None, 'shard')
- vector_second: float32 [5, 1024], P(None, 'shard')
- matrix_weights: bfloat16 [3, 1024, 1024], replicated
- vector_weights: bfloat16 [5, 1024], replicated
All inputs are finite; a program needn't handle non-finite values.
Results may differ from a plain program's by a relative error of at most 0.005.
Values may be sent and summed in bfloat16 or wider, within the bound.
A program may use at most 128 MiB of HBM per device.

v0:
```python
import jax
import jax.numpy as jnp
from jax import lax
from jax.sharding import PartitionSpec as P

STEP = 1000
beta_first = 0.9
beta_second = 0.999
learn_rate = 0.01
decay_rate = 0.1
epsilon = 1e-08


def adam_piece(total, master, moment, second, clip, decay):
    scaled = total * clip
    moment_next = beta_first * moment + (1.0 - beta_first) * scaled
    second_next = beta_second * second + (1.0 - beta_second) * scaled * scaled
    corrected = moment_next / (1.0 - beta_first**STEP)
    spread = jnp.sqrt(second_next / (1.0 - beta_second**STEP))
    update = corrected / (spread + epsilon)
    master_next = master - learn_rate * (update + decay * master)
    return (master_next, moment_next, second_next)


def squares_of(first, second):
    return jnp.sum(first * first) + jnp.sum(second * second)


def body(
    grads_matrix,
    grads_vector,
    master_matrix,
    master_vector,
    moment_matrix,
    moment_vector,
    second_matrix,
    second_vector,
):
    local_matrix = grads_matrix[0, 0].astype(jnp.float32)
    local_vector = grads_vector[0, 0].astype(jnp.float32)
    width = local_vector.shape[1]
    count = 3 * width * width + 5 * width
    part_matrix, part_vector = (
        lax.psum_scatter(
            local_matrix.astype(jnp.bfloat16), "shard", scatter_dimension=1, tiled=True
        ).astype(jnp.float32),
        lax.psum_scatter(
            local_vector.astype(jnp.bfloat16), "shard", scatter_dimension=1, tiled=True
        ).astype(jnp.float32),
    )
    mine_matrix, mine_vector = (
        lax.psum(part_matrix.astype(jnp.bfloat16), "rep").astype(jnp.float32),
        lax.psum(part_vector.astype(jnp.bfloat16), "rep").astype(jnp.float32),
    )
    squares = lax.psum(squares_of(mine_matrix, mine_vector), "shard")
    clip = jnp.minimum(1.0, 1.0 / jnp.sqrt(squares / count + 1e-06))
    master_mat, moment_mat, second_mat = adam_piece(
        mine_matrix, master_matrix, moment_matrix, second_matrix, clip, decay_rate
    )
    master_vec, moment_vec, second_vec = adam_piece(
        mine_vector, master_vector, moment_vector, second_vector, clip, 0.0
    )
    weights_mat, weights_vec = (
        lax.all_gather(master_mat.astype(jnp.bfloat16), "shard", axis=1, tiled=True),
        lax.all_gather(master_vec.astype(jnp.bfloat16), "shard", axis=1, tiled=True),
    )
    return (
        master_mat,
        master_vec,
        moment_mat,
        moment_vec,
        second_mat,
        second_vec,
        weights_mat,
        weights_vec,
    )


def solution(mesh):
    return jax.shard_map(
        body,
        mesh=mesh,
        in_specs=(
            P("rep", "shard", None, None, None),
            P("rep", "shard", None, None),
            P(None, "shard", None),
            P(None, "shard"),
            P(None, "shard", None),
            P(None, "shard"),
            P(None, "shard", None),
            P(None, "shard"),
        ),
        out_specs=(
            P(None, "shard", None),
            P(None, "shard"),
            P(None, "shard", None),
            P(None, "shard"),
            P(None, "shard", None),
            P(None, "shard"),
            P(),
            P(),
        ),
        check_vma=False,
    )
```

profile of v0, /device:TPU:0, one launch (start us, length us, event | category | flops | bytes accessed | tf_op | source)
XLA Modules:
  0.0 356.3 jit_solution(2101009983233991101)
XLA Ops:
  7.2 0.0 reduce-scatter.3.cloned.1.call-start
  7.2 0.7 reduce-scatter.3.cloned.1.call-update
  7.9 0.0 copy-start
  7.9 0.0 reduce-scatter.5.cloned.1.call-start
  8.0 0.7 reduce-scatter.5.cloned.1.call-update
  8.7 0.0 all-reduce.2.cloned.1.call-start
  8.7 115.1 %reduce-scatter.3.cloned.1.call-done = bf16[3,256,1024]{2,1,0:T(8,128)(2,1)} async-done(((bf16[3,1024,1024]{2,1,0:T(8,128)(2,1)}), bf16[3,256,1024]{2,1,0:T(8,128)(2,1)}) %reduce-scatter.3.cloned.1.call-update) | async-done | bytes 1572880 | tf_op jit(solution)/shard_map/reduce_scatter | solution.py:44
  123.8 0.0 all-reduce.2.cloned.1.call-update
  123.8 0.0 all-gather.2.cloned.1.call-start
  123.9 21.6 %reduce-scatter.5.cloned.1.call-done = bf16[5,256]{1,0:T(8,128)(2,1)} async-done(((bf16[5,1024]{1,0:T(8,128)(2,1)}), bf16[5,256]{1,0:T(8,128)(2,1)}) %reduce-scatter.5.cloned.1.call-update) | async-done | bytes 2576 | tf_op jit(solution)/shard_map/reduce_scatter | solution.py:47
  145.4 12.0 %psum.22 = bf16[5,256]{1,0:T(8,128)(2,1)S(1)} all-reduce(bf16[5,256]{1,0:T(8,128)(2,1)} %reduce-scatter.5.cloned.1.call-done), channel_id=1, replica_groups=mesh['rep'=8,'shard'=4] {'rep'}, use_global_device_ids=true, to_apply=%region_4.0 | all-reduce | flops 1280 | bytes 5120 | tf_op jit(solution)/shard_map/psum | solution.py:53
  157.5 0.6 fusion.6
  158.1 48.1 %all-reduce.2.cloned.1.call-done = bf16[3,256,1024]{2,1,0:T(8,128)(2,1)} async-done(((bf16[3,256,1024]{2,1,0:T(8,128)(2,1)}), bf16[3,256,1024]{2,1,0:T(8,128)(2,1)}) %all-reduce.2.cloned.1.call-update) | async-done | bytes 1572880 | tf_op jit(solution)/shard_map/psum | solution.py:52
  206.2 2.8 fusion.2
  210.3 12.3 %psum.23 = f32[]{:T(128)} all-reduce(f32[]{:T(128)S(6)} %add.46), channel_id=1, replica_groups=mesh['rep'=8,'shard'=4] {'shard'}, use_global_device_ids=true, to_apply=%region_6.0 | all-reduce | flops 1 | bytes 8 | tf_op jit(solution)/shard_map/psum | solution.py:55
  223.3 0.0 copy-done
  223.4 0.0 copy-start.1
  223.4 0.0 copy-start.2
  223.4 0.0 copy-start.3
  223.4 7.5 %fusion.11 = (bf16[3,256,1024]{2,1,0:T(8,128)(2,1)}, f32[3,256,1024]{2,1,0:T(8,128)}, f32[3,256,1024]{2,1,0:T(8,128)}, f32[3,256,1024]{2,1,0:T(8,128)}) fusion(f32[3,256,1024]{2,1,0:T(8,128)S(1)} %copy-done, f32[]{:T(128)S(6)} %min.3, bf16[3,256,1024]{2,1,0:T(8,128)(2,1)} %all-reduce.2.cloned.1.call-done, f32[3,256,1024]{2,1,0:T(8,128)} %param.14, ...), kind=kLoop, calls=%fused_computation.17 | loop fusion | flops 13369344 | bytes 22020100 | tf_op jit(solution)/shard_map/convert_element_type | solution.py:64
  230.9 0.0 all-gather.2.cloned.1.call-update
  230.9 0.0 copy-done.1
  230.9 0.0 copy-done.2
  230.9 0.0 copy-done.3
  231.0 0.6 fusion.8
  231.6 13.2 %all_gather.7 = bf16[5,1024]{1,0:T(8,128)(2,1)S(1)} all-gather(bf16[5,256]{1,0:T(8,128)(2,1)S(1)} %get-tuple-element.8), channel_id=1, replica_groups=mesh['rep'=8,'shard'=4] {'shard'}, dimensions={1}, use_global_device_ids=true | all-gather | bytes 12800 | tf_op jit(solution)/shard_map/all_gather | solution.py:65
  244.8 98.1 %all-gather.2.cloned.1.call-done = bf16[3,1024,1024]{2,1,0:T(8,128)(2,1)} async-done(((bf16[3,256,1024]{2,1,0:T(8,128)(2,1)}), bf16[3,1024,1024]{2,1,0:T(8,128)(2,1)}) %all-gather.2.cloned.1.call-update) | async-done | bytes 6291472 | tf_op jit(solution)/shard_map/all_gather | solution.py:64
  342.9 6.2 %copy.19 = bf16[3,1024,1024]{2,1,0:T(8,128)(2,1)} copy(bf16[3,1024,1024]{2,1,0:T(8,128)(2,1)} %all-gather.2.cloned.1.call-done) | data formatting | bytes 12582912
  349.1 0.6 copy.20
Async XLA Ops:
  7.2 116.6 %reduce-scatter.3.cloned.1.call-start = ((), (), s32[]{:S(2)}) async-start(), calls=%async_computation.2 | async-start | bytes 7864320 | tf_op jit(solution)/shard_map/reduce_scatter | solution.py:44
  7.9 215.5 %copy-start = (f32[3,256,1024]{2,1,0:T(8,128)S(1)}, f32[3,256,1024]{2,1,0:T(8,128)}, u32[]{:S(2)}) copy-start(f32[3,256,1024]{2,1,0:T(8,128)} %param.10) | copy-start | bytes 9437188
  7.9 137.5 %reduce-scatter.5.cloned.1.call-start = ((), (), s32[]{:S(2)}) async-start(), calls=%async_computation.4 | async-start | bytes 20480 | tf_op jit(solution)/shard_map/reduce_scatter | solution.py:47
  8.7 197.5 %all-reduce.2.cloned.1.call-start = ((), (), s32[]{:S(2)}) async-start(), calls=%async_computation.3 | async-start | bytes 3145728 | tf_op jit(solution)/shard_map/psum | solution.py:52
  123.8 219.1 %all-gather.2.cloned.1.call-start = ((), (), s32[]{:S(2)}) async-start(), calls=%async_computation.5 | async-start | bytes 7864320 | tf_op jit(solution)/shard_map/all_gather | solution.py:64
  223.4 7.6 %copy-start.1 = (f32[5,256]{1,0:T(8,128)S(1)}, f32[5,256]{1,0:T(8,128)}, u32[]{:S(2)}) copy-start(f32[5,256]{1,0:T(8,128)} %param.11) | copy-start | bytes 15364
  223.4 7.6 %copy-start.2 = (f32[5,256]{1,0:T(8,128)S(1)}, f32[5,256]{1,0:T(8,128)}, u32[]{:S(2)}) copy-start(f32[5,256]{1,0:T(8,128)} %param.15) | copy-start | bytes 15364
  223.4 7.6 %copy-start.3 = (f32[5,256]{1,0:T(8,128)S(1)}, f32[5,256]{1,0:T(8,128)}, u32[]{:S(2)}) copy-start(f32[5,256]{1,0:T(8,128)} %param.13) | copy-start | bytes 15364
Sparse Core Ops, SparseCore 0:
  10.3 113.4 reduce-scatter.2
  126.0 19.3 reduce-scatter.4
  149.0 57.1 all-reduce.1
  231.0 111.8 all-gather.1
where the time goes:
time: 357 us; the launch traced here: 356 us
  waiting for transfers between devices  284 us (80%)
  blocking collectives  37.6 us (11%)
  between operations  15.8 us (4%)
  other arithmetic  11.6 us (3%)
  local copies, waits for them, and re-layouts  6.82 us (2%)
    reduce_scatter x1, waiting for transfers between devices, body(): lax.psum_scatter(local_matrix.astype(jnp.bfloat16), 'shard', scatter_dime...  115 us
    all_gather x1, waiting for transfers between devices, body(): lax.all_gather(master_mat.astype(jnp.bfloat16), 'shard', axis=1, tiled=True)  98.1 us
    psum x1, waiting for transfers between devices, body(): lax.psum(part_matrix.astype(jnp.bfloat16), 'rep').astype(jnp.float32)  48.1 us
    reduce_scatter x1, waiting for transfers between devices, body(): lax.psum_scatter(local_vector.astype(jnp.bfloat16), 'shard', scatter_dime...  21.6 us
    all_gather x1, blocking collectives, body(): lax.all_gather(master_vec.astype(jnp.bfloat16), 'shard', axis=1, tiled=True)  13.2 us
    psum x1, blocking collectives, body(): squares = lax.psum(squares_of(mine_matrix, mine_vector), 'shard')  12.3 us
    psum x1, blocking collectives, body(): lax.psum(part_vector.astype(jnp.bfloat16), 'rep').astype(jnp.float32)  12 us
    convert_element_type x1, other arithmetic, body(): master_mat.astype(jnp.bfloat16)  7.51 us
  transfers between devices with their start and end apart: 4, of which 4 were waited for; matrix products, arithmetic and copies ran while one was open for 0% of the time, Pallas kernels for 0%

commit v1 on v0

--- a/solution.py
+++ b/solution.py
@@ -1,3 +1,4 @@
+import functools
 import jax
 import jax.numpy as jnp
 from jax import lax
@@ -9,6 +10,31 @@
 learn_rate = 0.01
 decay_rate = 0.1
 epsilon = 1e-08
+
+
+def use_samples(block_in, axis_id):
+    plain = lax.psum(1, axis_id)
+    inter, prior, h_now = (plain, lax.axis_index(axis_id), block_in.shape[1])
+    samples = [(k, (k + 1) % inter) for k in range(inter)]
+    in_order = [(k, (k - 1) % inter) for k in range(inter)]
+    near = jnp.zeros((*block_in.shape[:1], inter * h_now, *block_in.shape[2:]), block_in.dtype)
+    local_part = left_arr = block_in
+    r_now = inter // 2
+    near = lax.dynamic_update_slice_in_dim(near, block_in, prior * h_now, axis=1)
+    for c in range(1, r_now + 1):
+        local_part = lax.ppermute(local_part, axis_id, samples)
+        near = lax.dynamic_update_slice_in_dim(
+            near, local_part, (prior - c) % inter * h_now, axis=1
+        )
+        if c < inter - r_now:
+            left_arr = lax.ppermute(left_arr, axis_id, in_order)
+            near = lax.dynamic_update_slice_in_dim(
+                near, left_arr, (prior + c) % inter * h_now, axis=1
+            )
+    return near
+
+
+get_desk = functools.partial(use_samples, axis_id="shard")
 
 
 def adam_piece(total, master, moment, second, clip, decay):
@@ -61,7 +87,7 @@
         mine_vector, master_vector, moment_vector, second_vector, clip, 0.0
     )
     weights_mat, weights_vec = (
-        lax.all_gather(master_mat.astype(jnp.bfloat16), "shard", axis=1, tiled=True),
+        get_desk(master_mat.astype(jnp.bfloat16)),
         lax.all_gather(master_vec.astype(jnp.bfloat16), "shard", axis=1, tiled=True),
     )
     return (

time: 357 us -> 357 us (level)
  waiting for transfers between devices: 284 us -> 222 us
  blocking collectives: 37.6 us -> 94.1 us
  starting transfers between devices: 0.15 us -> 3.94 us
    all_gather x1 -> x0, waiting for transfers between devices: 98.1 us -> none  [body(): lax.all_gather(master_mat.astype(jnp.bfloat16), 'shard', axis=1, tiled=True)]
    all_gather x1, blocking collectives: 13.2 us -> 69.7 us  [body(): lax.all_gather(master_vec.astype(jnp.bfloat16), 'shard', axis=1, tiled=True)]
    ppermute x0 -> x3, waiting for transfers between devices: none -> 35.5 us  [the longest x2 35.5 us: use_samples(): local_part = lax.ppermute(local_part, axis_id, samples)]
    convert_element_type x1 -> x0, other arithmetic: 7.51 us -> none  [body(): master_mat.astype(jnp.bfloat16)]
    dynamic_update_slice x0 -> x1, other arithmetic: none -> 7.3 us  [use_samples(): lax.dynamic_update_slice_in_dim(near, block_in, prior * h_now, axis=1)]
    unnamed x10 -> x13, local copies, waits for them, and re-layouts: 6.82 us -> 0.81 us
    dynamic_update_slice x0 -> x3, local copies, waits for them, and re-layouts: none -> 5.19 us  [the longest x1 2.67 us: use_samples(): lax.dynamic_update_slice_in_dim(near, left_arr, (prior + c) % inter * h_n...]
    ppermute x0 -> x3, starting transfers between devices: none -> 3.83 us  [the longest x1 3.82 us: use_samples(): left_arr = lax.ppermute(left_arr, axis_id, in_order)]
  transfers between devices with their start and end apart: 4 -> 6, of which waited for: 4 -> 4; matrix products, arithmetic and copies ran while one was open for 0% -> 1% of each run, Pallas kernels for 0% -> 0%
where the time goes in v1:
time: 357 us
  waiting for transfers between devices  222 us (62%)
  blocking collectives  94.1 us (26%)
  between operations  15.8 us (4%)
  other arithmetic  11.5 us (3%)
  local copies, waits for them, and re-layouts  9.6 us (3%)
  starting transfers between devices  3.94 us (1%)
    reduce_scatter x1, waiting for transfers between devices, body(): lax.psum_scatter(local_matrix.astype(jnp.bfloat16), 'shard', scatter_dime...  115 us
    all_gather x1, blocking collectives, body(): lax.all_gather(master_vec.astype(jnp.bfloat16), 'shard', axis=1, tiled=True)  69.7 us
    psum x1, waiting for transfers between devices, body(): lax.psum(part_matrix.astype(jnp.bfloat16), 'rep').astype(jnp.float32)  48.1 us
    ppermute x2, waiting for transfers between devices, use_samples(): local_part = lax.ppermute(local_part, axis_id, samples)  35.5 us
    reduce_scatter x1, waiting for transfers between devices, body(): lax.psum_scatter(local_vector.astype(jnp.bfloat16), 'shard', scatter_dime...  21.6 us
    psum x1, blocking collectives, body(): squares = lax.psum(squares_of(mine_matrix, mine_vector), 'shard')  12.3 us
    psum x1, blocking collectives, body(): lax.psum(part_vector.astype(jnp.bfloat16), 'rep').astype(jnp.float32)  12 us
    dynamic_update_slice x1, other arithmetic, use_samples(): lax.dynamic_update_slice_in_dim(near, block_in, prior * h_now, axis=1)  7.3 us
  transfers between devices with their start and end apart: 6, of which 4 were waited for; matrix products, arithmetic and copies ran while one was open for 1% of the time, Pallas kernels for 0%

profile of v1, /device:TPU:0, one launch (start us, length us, event | category | flops | bytes accessed | tf_op | source)
XLA Modules:
  0.0 356.7 jit_solution(16911491516338478768)
XLA Ops:
  7.2 0.0 reduce-scatter.3.cloned.1.call-start
  7.2 0.7 reduce-scatter.3.cloned.1.call-update
  7.9 0.0 reduce-scatter.5.cloned.1.call-start
  7.9 0.7 reduce-scatter.5.cloned.1.call-update
  8.6 0.0 all-reduce.2.cloned.1.call-start
  8.7 115.1 %reduce-scatter.3.cloned.1.call-done = bf16[3,256,1024]{2,1,0:T(8,128)(2,1)} async-done(((bf16[3,1024,1024]{2,1,0:T(8,128)(2,1)}), bf16[3,256,1024]{2,1,0:T(8,128)(2,1)}) %reduce-scatter.3.cloned.1.call-update) | async-done | bytes 1572880 | tf_op jit(solution)/shard_map/reduce_scatter | solution.py:70
  123.8 0.0 all-reduce.2.cloned.1.call-update
  123.8 21.6 %reduce-scatter.5.cloned.1.call-done = bf16[5,256]{1,0:T(8,128)(2,1)} async-done(((bf16[5,1024]{1,0:T(8,128)(2,1)}), bf16[5,256]{1,0:T(8,128)(2,1)}) %reduce-scatter.5.cloned.1.call-update) | async-done | bytes 2576 | tf_op jit(solution)/shard_map/reduce_scatter | solution.py:73
  145.4 12.0 %psum.22 = bf16[5,256]{1,0:T(8,128)(2,1)S(1)} all-reduce(bf16[5,256]{1,0:T(8,128)(2,1)} %reduce-scatter.5.cloned.1.call-done), channel_id=1, replica_groups=mesh['rep'=8,'shard'=4] {'rep'}, use_global_device_ids=true, to_apply=%region_4.0 | all-reduce | flops 1280 | bytes 5120 | tf_op jit(solution)/shard_map/psum | solution.py:79
  157.5 0.6 fusion.6
  158.1 48.1 %all-reduce.2.cloned.1.call-done = bf16[3,256,1024]{2,1,0:T(8,128)(2,1)} async-done(((bf16[3,256,1024]{2,1,0:T(8,128)(2,1)}), bf16[3,256,1024]{2,1,0:T(8,128)(2,1)}) %all-reduce.2.cloned.1.call-update) | async-done | bytes 1572880 | tf_op jit(solution)/shard_map/psum | solution.py:78
  206.2 0.0 copy-start.2
  206.2 3.0 fusion.2
  210.5 12.3 %psum.23 = f32[]{:T(128)} all-reduce(f32[]{:T(128)S(6)} %add.73), channel_id=1, replica_groups=mesh['rep'=8,'shard'=4] {'shard'}, use_global_device_ids=true, to_apply=%region_6.0 | all-reduce | flops 1 | bytes 8 | tf_op jit(solution)/shard_map/psum | solution.py:81
  223.5 0.0 copy-start
  223.5 0.0 copy-start.1
  223.5 3.6 %broadcast_in_dim.3 = bf16[3,1024,1024]{2,1,0:T(8,128)(2,1)} broadcast(bf16[]{:T(256)} %constant.64.clone.1), dimensions={} | broadcast | bytes 6291458 | tf_op jit(solution)/shard_map/broadcast_in_dim | solution.py:20
  227.1 0.0 copy-done.2
  227.1 0.0 copy-done
  227.1 0.2 copy-done.1
  227.3 0.0 copy-start.3
  227.3 0.0 copy-start.4
  227.3 0.0 copy-start.5
  227.3 7.3 %constant_dynamic-update-slice_fusion.3 = (bf16[3,1024,1024]{2,1,0:T(8,128)(2,1)}, bf16[3,256,1024]{2,1,0:T(8,128)(2,1)}, f32[3,256,1024]{2,1,0:T(8,128)}, f32[3,256,1024]{2,1,0:T(8,128)}, f32[3,256,1024]{2,1,0:T(8,128)}) fusion(bf16[3,1024,1024]{2,1,0:T(8,128)(2,1)} %broadcast_in_dim.3, s32[]{:T(128)S(6)} %select_n.27, f32[3,256,1024]{2,1,0:T(8,128)S(1)} %copy-done.1, ...), kind=kLoop, calls=%fused_computation.19 | loop fusion | flops 13369344 | bytes 23592968 | tf_op jit(solution)/shard_map/dynamic_update_slice | solution.py:23
  234.6 0.0 collective-permute-start
  234.6 3.8 %collective-permute-start.1 = (bf16[3,256,1024]{2,1,0:T(8,128)(2,1)}, bf16[3,256,1024]{2,1,0:T(8,128)(2,1)}, u32[]{:S(2)}, u32[]{:S(2)}) collective-permute-start(bf16[3,256,1024]{2,1,0:T(8,128)(2,1)} %get-tuple-element.13), channel_id=1, source_target_pairs={{0,3},{1,0},{2,1},{3,2},{4,7},{5,4},{6,5},{7,6},{8,11},{9,8},{10,9... | collective-permute-start | bytes 4718600 | tf_op jit(solution)/shard_map/ppermute | solution.py:30
  238.4 35.5 %collective-permute-done = bf16[3,256,1024]{2,1,0:T(8,128)(2,1)S(1)} collective-permute-done((bf16[3,256,1024]{2,1,0:T(8,128)(2,1)}, bf16[3,256,1024]{2,1,0:T(8,128)(2,1)S(1)}, u32[]{:S(2)}, u32[]{:S(2)}) %collective-permute-start) | collective-permute-done | bytes 1572896 | tf_op jit(solution)/shard_map/ppermute | solution.py:25
  274.0 0.0 collective-permute-start.2
  274.0 0.0 copy-done.3
  274.0 0.0 copy-done.4
  274.0 0.0 copy-done.5
  274.0 0.6 fusion.8
  274.6 69.7 %all_gather.3 = bf16[5,1024]{1,0:T(8,128)(2,1)S(1)} all-gather(bf16[5,256]{1,0:T(8,128)(2,1)S(1)} %get-tuple-element.8), channel_id=1, replica_groups=mesh['rep'=8,'shard'=4] {'shard'}, dimensions={1}, use_global_device_ids=true | all-gather | bytes 12800 | tf_op jit(solution)/shard_map/all_gather | solution.py:91
  344.3 1.3 constant_dynamic-update-slice_fusion.2
  345.6 0.0 collective-permute-done.1
  345.6 2.7 constant_dynamic-update-slice_fusion.1
  348.3 0.0 collective-permute-done.2
  348.3 1.3 constant_dynamic-update-slice_fusion
  349.5 0.6 copy.22
Async XLA Ops:
  7.2 116.6 %reduce-scatter.3.cloned.1.call-start = ((), (), s32[]{:S(2)}) async-start(), calls=%async_computation.2 | async-start | bytes 7864320 | tf_op jit(solution)/shard_map/reduce_scatter | solution.py:70
  7.9 137.5 %reduce-scatter.5.cloned.1.call-start = ((), (), s32[]{:S(2)}) async-start(), calls=%async_computation.4 | async-start | bytes 20480 | tf_op jit(solution)/shard_map/reduce_scatter | solution.py:73
  8.6 197.5 %all-reduce.2.cloned.1.call-start = ((), (), s32[]{:S(2)}) async-start(), calls=%async_computation.3 | async-start | bytes 3145728 | tf_op jit(solution)/shard_map/psum | solution.py:78
  206.2 20.9 %copy-start.2 = (f32[3,256,1024]{2,1,0:T(8,128)S(1)}, f32[3,256,1024]{2,1,0:T(8,128)}, u32[]{:S(2)}) copy-start(f32[3,256,1024]{2,1,0:T(8,128)} %param.14) | copy-start | bytes 9437188
  223.5 3.6 %copy-start = (bf16[3,256,1024]{2,1,0:T(8,128)(2,1)S(1)}, bf16[3,256,1024]{2,1,0:T(8,128)(2,1)}, u32[]{:S(2)}) copy-start(bf16[3,256,1024]{2,1,0:T(8,128)(2,1)} %all-reduce.2.cloned.1.call-done) | copy-start | bytes 4718596
  223.5 3.8 %copy-start.1 = (f32[3,256,1024]{2,1,0:T(8,128)S(1)}, f32[3,256,1024]{2,1,0:T(8,128)}, u32[]{:S(2)}) copy-start(f32[3,256,1024]{2,1,0:T(8,128)} %param.10) | copy-start | bytes 9437188
  227.3 46.7 %copy-start.3 = (f32[5,256]{1,0:T(8,128)S(1)}, f32[5,256]{1,0:T(8,128)}, u32[]{:S(2)}) copy-start(f32[5,256]{1,0:T(8,128)} %param.11) | copy-start | bytes 15364
  227.3 46.7 %copy-start.4 = (f32[5,256]{1,0:T(8,128)S(1)}, f32[5,256]{1,0:T(8,128)}, u32[]{:S(2)}) copy-start(f32[5,256]{1,0:T(8,128)} %param.15) | copy-start | bytes 15364
  227.3 46.7 %copy-start.5 = (f32[5,256]{1,0:T(8,128)S(1)}, f32[5,256]{1,0:T(8,128)}, u32[]{:S(2)}) copy-start(f32[5,256]{1,0:T(8,128)} %param.13) | copy-start | bytes 15364
  234.6 39.3 %collective-permute-start = (bf16[3,256,1024]{2,1,0:T(8,128)(2,1)}, bf16[3,256,1024]{2,1,0:T(8,128)(2,1)S(1)}, u32[]{:S(2)}, u32[]{:S(2)}) collective-permute-start(bf16[3,256,1024]{2,1,0:T(8,128)(2,1)} %get-tuple-element.13), channel_id=1, source_target_pairs={{0,1},{1,2},{2,3},{3,0},{4,5},{5,6},{6,7},{7,4},{8,9},{9,10},{10,1... | collective-permute-start | bytes 4718600 | tf_op jit(solution)/shard_map/ppermute | solution.py:25
  234.6 111.0 %collective-permute-start.1 = (bf16[3,256,1024]{2,1,0:T(8,128)(2,1)}, bf16[3,256,1024]{2,1,0:T(8,128)(2,1)}, u32[]{:S(2)}, u32[]{:S(2)}) collective-permute-start(bf16[3,256,1024]{2,1,0:T(8,128)(2,1)} %get-tuple-element.13), channel_id=1, source_target_pairs={{0,3},{1,0},{2,1},{3,2},{4,7},{5,4},{6,5},{7,6},{8,11},{9,8},{10,9... | collective-permute-start | bytes 4718600 | tf_op jit(solution)/shard_map/ppermute | solution.py:30
  274.0 74.3 %collective-permute-start.2 = (bf16[3,256,1024]{2,1,0:T(8,128)(2,1)S(1)}, bf16[3,256,1024]{2,1,0:T(8,128)(2,1)S(1)}, u32[]{:S(2)}, u32[]{:S(2)}) collective-permute-start(bf16[3,256,1024]{2,1,0:T(8,128)(2,1)S(1)} %collective-permute-done), channel_id=1, source_target_pairs={{0,1},{1,2},{2,3},{3,0},{4,5},{5,6},{6,7},{7,4},{8,9},{9,10},{10,1... | collective-permute-start | bytes 4718600 | tf_op jit(solution)/shard_map/ppermute | solution.py:25
Sparse Core Ops, SparseCore 0:
  10.3 113.4 reduce-scatter.2
  126.0 19.3 reduce-scatter.4
  149.0 57.1 all-reduce.1
